TPU v7x, 32 devices: a whole 2x2x4 slice. The times are simulated.
32 devices in a mesh: groups: 2 (over y), dp: 4 (over z), tensor: 2 (over x), sub: 2 (over core).
Axes of the slice: x: 2, y: 2, z: 4, core: 2. Of those that a mesh axis runs over, the one named last changes fastest.
Arguments:
- token_input: bfloat16 [16, 16, 8192], P('dp', 'groups', ('tensor', 'sub')), parts along dimension 1, may hold values from -6 to 6
- gate_input: bfloat16 [16, 16, 8192], P('dp', 'groups', ('tensor', 'sub')), parts along dimension 1, may hold values from -6 to 6
- conv_taps: bfloat16 [16, 16, 3, 8192], P('dp', 'groups', None, ('tensor', 'sub')), parts along dimension 1, may hold values from -6 to 6
- scan_state: bfloat16 [16, 16, 16, 8192], P('dp', 'groups', None, ('tensor', 'sub')), parts along dimension 1, may hold values from -6 to 6
- conv_weight: bfloat16 [4, 8192], P(None, ('tensor', 'sub')), may hold values from -3 to 3
- conv_bias: float32 [8192], P(('tensor', 'sub')), may hold values from -3 to 3
- select_weight: bfloat16 [8192, 544], P(('tensor', 'sub')), may hold values from -0.0625 to 0.0625
- step_gain: float32 [512], replicated, may hold values from 0.1 to 1.9
- step_weight: bfloat16 [512, 8192], P(None, ('tensor', 'sub')), may hold values from -0.25 to 0.25
- step_bias: float32 [8192], P(('tensor', 'sub')), may hold values from -4.5 to -1
- decay_log: float32 [16, 8192], P(None, ('tensor', 'sub')), may hold values from 0 to 2.8
- skip_gain: float32 [8192], P(('tensor', 'sub')), may hold values from 0 to 2
- query: bfloat16 [16, 16, 8192], P('dp', ('groups', 'sub'), 'tensor'), parts along dimension 1, may hold values from -8 to 8
- fresh_key: bfloat16 [16, 16, 1024], P('dp', ('groups', 'sub'), 'tensor'), parts along dimension 1, may hold values from -6 to 6
- fresh_value: bfloat16 [16, 16, 1024], P('dp', ('groups', 'sub'), 'tensor'), parts along dimension 1, may hold values from -6 to 6
- key_cache: bfloat16 [16, 16, 256, 1024], P('dp', ('groups', 'sub'), None, 'tensor'), parts along dimension 1, may hold values from -6 to 6
- value_cache: bfloat16 [16, 16, 256, 1024], P('dp', ('groups', 'sub'), None, 'tensor'), parts along dimension 1, may hold values from -6 to 6
- cache_lengths: int32 [16, 16], P(None, 'groups'), parts along dimension 1, may hold values from 2 to 256, as said below
- parents: int32 [16, 16], P('groups'), parts along dimension 0, may hold values from 0 to 15
Outputs:
- next_state: bfloat16 [16, 16, 16, 8192], P('dp', 'groups', None, ('tensor', 'sub')), parts along dimension 1
- next_taps: bfloat16 [16, 16, 3, 8192], P('dp', 'groups', None, ('tensor', 'sub')), parts along dimension 1
- mamba_output: bfloat16 [16, 16, 8192], P('dp', 'groups', ('tensor', 'sub')), parts along dimension 1
- attention_output: bfloat16 [16, 16, 8192], P('dp', ('groups', 'sub'), 'tensor'), parts along dimension 1
There are 2 independent parts, one for each index of `groups`. A program takes and returns all parts, laid end to end along the dimension named above; an argument that names none is the same for every part. Nothing has to cross between parts.
Inputs may be any that keep to these rules, and one draw needn't show every extreme that they name: cache_lengths[b, p] counts the live cache positions of beam b of prompt p, which are its first positions; in every draw some beam has all 256.
All inputs are finite; a program needn't handle non-finite values.
Results may differ from a plain program's by a relative error of at most 0.005.
Values may be sent and summed in bfloat16 or wider, within the bound.
No kernel may reach another device: no remote copies, remote signals or barrier semaphores. Data moves between devices by JAX's collectives and lax.ppermute only.
A program may use at most 128 MiB of HBM per device.

v0:
```python
import jax
import jax.numpy as jnp
from jax import lax
from jax.sharding import PartitionSpec as P

HEADS = 64
KV_HEADS = 8
HEAD_DIM = 128


big_negative = -1e30


def choose_rows(array, picks):
    index = picks.reshape(picks.shape + (1,) * (array.ndim - 2))
    return jnp.take_along_axis(array, index, axis=0)


def parent_rows(parents, first, count):
    return lax.dynamic_slice_in_dim(parents, first, count, 0).T


def body(
    token_input,
    gate_input,
    conv_taps,
    scan_state,
    conv_weight,
    conv_bias,
    select_weight,
    step_gain,
    step_weight,
    step_bias,
    decay_log,
    skip_gain,
    query,
    fresh_key,
    fresh_value,
    key_cache,
    value_cache,
    cache_lengths,
    parents,
):
    group_width = lax.axis_size("dp")
    my_index = lax.axis_index("dp")
    sub_index = lax.axis_index("sub")
    beam_slots = token_input.shape[0]
    prompt_count = token_input.shape[1]
    prompt_share = prompt_count // group_width
    cache_prompts = key_cache.shape[1]
    cache_share = cache_prompts // group_width
    cache_base = sub_index * cache_prompts
    cache_length = key_cache.shape[2]
    group_size = HEADS // KV_HEADS
    score_scale = HEAD_DIM ** (-0.5)
    heads_local = query.shape[2] // HEAD_DIM
    kv_local = fresh_key.shape[2] // HEAD_DIM
    state_picks = parent_rows(parents, my_index * prompt_share, prompt_share)
    cache_picks = parent_rows(parents, cache_base + my_index * cache_share, cache_share)
    local_lengths = lax.dynamic_slice_in_dim(cache_lengths, cache_base, cache_prompts, 1)
    prompt_parents = parent_rows(parents, cache_base, cache_prompts)
    positions = jnp.arange(cache_length, dtype=jnp.int32)
    arrived = (
        lax.all_to_all(conv_taps, "dp", split_axis=1, concat_axis=0, tiled=True),
        lax.all_to_all(scan_state, "dp", split_axis=1, concat_axis=0, tiled=True),
        lax.all_to_all(key_cache, "dp", split_axis=1, concat_axis=0, tiled=True),
        lax.all_to_all(value_cache, "dp", split_axis=1, concat_axis=0, tiled=True),
    )
    parent_taps, parent_state, parent_keys, parent_values = (
        lax.all_to_all(
            choose_rows(arrived[0], state_picks), "dp", split_axis=0, concat_axis=1, tiled=True
        ),
        lax.all_to_all(
            choose_rows(arrived[1], state_picks), "dp", split_axis=0, concat_axis=1, tiled=True
        ),
        lax.all_to_all(
            choose_rows(arrived[2], cache_picks), "dp", split_axis=0, concat_axis=1, tiled=True
        ),
        lax.all_to_all(
            choose_rows(arrived[3], cache_picks), "dp", split_axis=0, concat_axis=1, tiled=True
        ),
    )
    children = lax.dynamic_slice_in_dim(prompt_parents, my_index * beam_slots, beam_slots, 0)
    parent_length = jnp.take_along_axis(local_lengths, children, axis=0)
    queries = query.reshape((beam_slots, cache_prompts, kv_local, group_size, HEAD_DIM))
    new_keys = fresh_key.reshape((beam_slots, cache_prompts, kv_local, HEAD_DIM))
    new_values = fresh_value.reshape((beam_slots, cache_prompts, kv_local, HEAD_DIM))
    keys_split = parent_keys.reshape((beam_slots, cache_prompts, cache_length, kv_local, HEAD_DIM))
    values_split = parent_values.reshape(
        (beam_slots, cache_prompts, cache_length, kv_local, HEAD_DIM)
    )
    scores = (
        jnp.einsum("rpkgd,rptkd->rpkgt", queries, keys_split, preferred_element_type=jnp.float32)
        * score_scale
    )
    live_mask = positions[None, None, None, None, :] < parent_length[:, :, None, None, None]
    fresh_score = (
        jnp.einsum("rpkgd,rpkd->rpkg", queries, new_keys, preferred_element_type=jnp.float32)
        * score_scale
    )
    row_max = jnp.maximum(jnp.max(jnp.where(live_mask, scores, big_negative), axis=-1), fresh_score)
    weights = jnp.where(live_mask, jnp.exp(scores - row_max[..., None]), 0.0)
    fresh_weight = jnp.exp(fresh_score - row_max)
    row_total = jnp.sum(weights, axis=-1) + fresh_weight
    weights_half = (weights / row_total[..., None]).astype(jnp.bfloat16)
    fresh_half = (fresh_weight / row_total).astype(jnp.bfloat16)
    attended = jnp.einsum(
        "rpkgt,rptkd->rpkgd", weights_half, values_split, preferred_element_type=jnp.float32
    )
    attended = (
        attended
        + fresh_half.astype(jnp.float32)[..., None]
        * new_values.astype(jnp.float32)[:, :, :, None, :]
    )
    attention_output = attended.reshape((beam_slots, cache_prompts, heads_local * HEAD_DIM)).astype(
        jnp.bfloat16
    )
    window = jnp.concatenate([parent_taps, token_input[:, :, None, :]], axis=2)
    conv_output = jax.nn.silu(
        jnp.sum(window.astype(jnp.float32) * conv_weight.astype(jnp.float32), axis=2) + conv_bias
    )
    conv_half = conv_output.astype(jnp.bfloat16)
    partial_sums = jnp.einsum(
        "bpc,cr->bpr", conv_half, select_weight, preferred_element_type=jnp.float32
    )
    projected = lax.psum(partial_sums, ("tensor", "sub"))
    rank_size = step_gain.shape[0]
    state_size = decay_log.shape[0]
    step_raw = projected[..., :rank_size]
    state_input = projected[..., rank_size : rank_size + state_size]
    state_readout = projected[..., rank_size + state_size :]
    step_norm = (
        step_raw
        * lax.rsqrt(jnp.mean(step_raw * step_raw, axis=-1, keepdims=True) + 1e-06)
        * step_gain
    ).astype(jnp.bfloat16)
    step_size = jax.nn.softplus(
        jnp.einsum("bpr,rc->bpc", step_norm, step_weight, preferred_element_type=jnp.float32)
        + step_bias
    )
    decay_factor = jnp.exp(-step_size[:, :, None, :] * jnp.exp(decay_log)[None, None])
    state_next = (
        decay_factor * parent_state.astype(jnp.float32)
        + step_size[:, :, None, :] * state_input[..., None] * conv_output[:, :, None, :]
    )
    readout = jnp.sum(state_readout[..., None] * state_next, axis=2) + skip_gain * conv_output
    mamba_output = (readout * jax.nn.silu(gate_input.astype(jnp.float32))).astype(jnp.bfloat16)
    return (state_next.astype(jnp.bfloat16), window[:, :, 1:, :], mamba_output, attention_output)


def solution(mesh):
    placed = (
        P("dp", "groups", ("tensor", "sub")),
        P("dp", "groups", ("tensor", "sub")),
        P("dp", "groups", None, ("tensor", "sub")),
        P("dp", "groups", None, ("tensor", "sub")),
        P(None, ("tensor", "sub")),
        P(("tensor", "sub")),
        P(("tensor", "sub"), None),
        P(),
        P(None, ("tensor", "sub")),
        P(("tensor", "sub")),
        P(None, ("tensor", "sub")),
        P(("tensor", "sub")),
        P("dp", ("groups", "sub"), "tensor"),
        P("dp", ("groups", "sub"), "tensor"),
        P("dp", ("groups", "sub"), "tensor"),
        P("dp", ("groups", "sub"), None, "tensor"),
        P("dp", ("groups", "sub"), None, "tensor"),
        P(None, "groups"),
        P("groups", None),
    )
    return jax.shard_map(
        body,
        mesh=mesh,
        in_specs=placed,
        out_specs=(
            P("dp", "groups", None, ("tensor", "sub")),
            P("dp", "groups", None, ("tensor", "sub")),
            P("dp", "groups", ("tensor", "sub")),
            P("dp", ("groups", "sub"), "tensor"),
        ),
        check_vma=False,
    )
```

profile of v0, /device:TPU:0, one launch (start us, length us, event | category | flops | bytes accessed | tf_op | source)
XLA Modules:
  0.0 556.5 jit_solution(12656276790948650497)
XLA Ops:
  7.2 2.2 copy.165
  9.4 6.3 %all-to-all-start = ((bf16[4,8,3,2048]{3,0,2,1:T(4,128)(2,1)}), bf16[4,8,3,2048]{3,0,2,1:T(4,128)(2,1)S(1)}, u32[]{:S(2)}, u32[]{:S(2)}) async-start(bf16[4,8,3,2048]{3,0,2,1:T(4,128)(2,1)} %copy.165), calls=%async_computation | async-start | bytes 786432 | tf_op jit(solution)/shard_map/all_to_all | solution.py:64
  17.4 10.0 %all-to-all-done = bf16[4,8,3,2048]{3,0,2,1:T(4,128)(2,1)S(1)} async-done(((bf16[4,8,3,2048]{3,0,2,1:T(4,128)(2,1)}), bf16[4,8,3,2048]{3,0,2,1:T(4,128)(2,1)S(1)}, u32[]{:S(2)}, u32[]{:S(2)}) %all-to-all-start) | async-done | bytes 393248 | tf_op jit(solution)/shard_map/all_to_all | solution.py:64
  30.4 3.5 all-to-all-start.1
  33.9 3.2 copy.174
  37.1 7.7 %all-to-all-done.1 = bf16[16,2,3,2048]{3,1,2,0:T(2,128)(2,1)S(1)} async-done(((bf16[16,2,3,2048]{3,1,2,0:T(2,128)(2,1)}), bf16[16,2,3,2048]{3,1,2,0:T(2,128)(2,1)S(1)}, u32[]{:S(2)}, u32[]{:S(2)}) %all-to-all-start.1) | async-done | bytes 393248 | tf_op jit(solution)/shard_map/all_to_all | solution.py:70
  44.8 4.5 all-to-all-start.2
  49.3 4.6 copy.185
  53.8 41.7 %all-to-all-done.2 = bf16[4,8,16,2048]{3,2,0,1:T(8,128)(2,1)} async-done(((bf16[4,8,16,2048]{3,2,0,1:T(8,128)(2,1)}), bf16[4,8,16,2048]{3,2,0,1:T(8,128)(2,1)}, u32[]{:S(2)}, u32[]{:S(2)}) %all-to-all-start.2) | async-done | bytes 2097184 | tf_op jit(solution)/shard_map/all_to_all | solution.py:65
  95.5 4.9 all-to-all-start.4
  100.4 4.5 copy.189
  104.9 88.1 %all-to-all-done.4 = bf16[4,4,256,512]{3,2,0,1:T(8,128)(2,1)} async-done(((bf16[4,4,256,512]{3,2,0,1:T(8,128)(2,1)}), bf16[4,4,256,512]{3,2,0,1:T(8,128)(2,1)}, u32[]{:S(2)}, u32[]{:S(2)}) %all-to-all-start.4) | async-done | bytes 4194336 | tf_op jit(solution)/shard_map/all_to_all | solution.py:66
  193.1 4.9 all-to-all-start.6
  198.0 3.2 copy.176
  201.1 3.6 gather_fusion.1
  204.7 3.2 broadcast_select_fusion
  207.9 82.8 %all-to-all-done.6 = bf16[4,4,256,512]{3,2,0,1:T(8,128)(2,1)} async-done(((bf16[4,4,256,512]{3,2,0,1:T(8,128)(2,1)}), bf16[4,4,256,512]{3,2,0,1:T(8,128)(2,1)}, u32[]{:S(2)}, u32[]{:S(2)}) %all-to-all-start.6) | async-done | bytes 4194336 | tf_op jit(solution)/shard_map/all_to_all | solution.py:67
  290.6 4.5 all-to-all-start.3
  295.2 5.0 gather_fusion.3
  300.2 4.9 gather_fusion.4
  305.1 7.5 %fusion.1 = (bf16[16,1,256,512]{3,2,1,0:T(8,128)(2,1)}, bf16[16,1,256,512]{3,2,1,0:T(8,128)(2,1)}) fusion(bf16[16,256,512]{2,1,0:T(8,128)(2,1)} %gather_fusion.3, pred[16]{0:T(512)(128)(4,1)S(1)} %and_bitcast_fusion, bf16[16,256,512]{2,1,0:T(8,128)(2,1)} %gather_fusion.4), kind=kLoop, calls=%fused_computation.8 | loop fusion | flops 4194304 | bytes 16777232 | tf_op jit(solution)/shard_map/jit(take_along_axis)/select_n | solution.py:16
  312.6 30.2 %all-to-all-done.3 = bf16[16,2,16,2048]{3,2,1,0:T(8,128)(2,1)} async-done(((bf16[16,2,16,2048]{3,2,1,0:T(8,128)(2,1)}), bf16[16,2,16,2048]{3,2,1,0:T(8,128)(2,1)}, u32[]{:S(2)}, u32[]{:S(2)}) %all-to-all-start.3) | async-done | bytes 2097184 | tf_op jit(solution)/shard_map/all_to_all | solution.py:73
  342.9 4.9 all-to-all-start.5
  348.0 92.5 %all-to-all-done.5 = bf16[16,1,256,512]{3,2,1,0:T(8,128)(2,1)} async-done(((bf16[16,1,256,512]{3,2,1,0:T(8,128)(2,1)}), bf16[16,1,256,512]{3,2,1,0:T(8,128)(2,1)}, u32[]{:S(2)}, u32[]{:S(2)}) %all-to-all-start.5) | async-done | bytes 4194336 | tf_op jit(solution)/shard_map/all_to_all | solution.py:76
  440.5 5.0 all-to-all-start.7
  453.1 28.8 %all-reduce.2.cloned.1.call-done = f32[4,8,544]{2,1,0:T(8,128)} async-done(((f32[4,8,544]{2,1,0:T(8,128)}), f32[4,8,544]{2,1,0:T(8,128)}) %all-reduce.2.cloned.1.call-update) | async-done | bytes 69648 | tf_op jit(solution)/shard_map/psum | solution.py:126
  487.6 4.4 multiply_reduce_fusion
  500.7 7.3 %copy.187 = bf16[4,4,1,256,512]{3,4,1,0,2:T(8,128)(2,1)} copy(bf16[4,4,1,256,512]{4,3,0,1,2:T(8,128)(2,1)} %bitcast.36) | data formatting | bytes 8388608 | tf_op jit(solution)/shard_map/all_to_all | solution.py:76
  508.0 2.9 select_reduce_fusion
  511.3 26.9 %all-to-all-done.7 = bf16[16,1,256,512]{3,2,1,0:T(8,128)(2,1)} async-done(((bf16[16,1,256,512]{3,2,1,0:T(8,128)(2,1)}), bf16[16,1,256,512]{3,2,1,0:T(8,128)(2,1)}, u32[]{:S(2)}, u32[]{:S(2)}) %all-to-all-start.7) | async-done | bytes 4194336 | tf_op jit(solution)/shard_map/all_to_all | solution.py:79
  538.2 7.3 %copy.191 = bf16[4,4,1,256,512]{3,4,1,0,2:T(8,128)(2,1)} copy(bf16[4,4,1,256,512]{4,3,0,1,2:T(8,128)(2,1)} %bitcast.50) | data formatting | bytes 8388608 | tf_op jit(solution)/shard_map/all_to_all | solution.py:79
  545.5 3.4 fusion.5
  (90 shorter events, 27.8 us)
Async XLA Ops:
  7.2 442.2 %copy-start = (bf16[2048,544]{0,1:T(8,128)(2,1)S(1)}, bf16[2048,544]{0,1:T(8,128)(2,1)}, u32[]{:S(2)}) copy-start(bf16[2048,544]{0,1:T(8,128)(2,1)} %param.27) | copy-start | bytes 6684676
  9.4 18.0 %all-to-all-start = ((bf16[4,8,3,2048]{3,0,2,1:T(4,128)(2,1)}), bf16[4,8,3,2048]{3,0,2,1:T(4,128)(2,1)S(1)}, u32[]{:S(2)}, u32[]{:S(2)}) async-start(bf16[4,8,3,2048]{3,0,2,1:T(4,128)(2,1)} %copy.165), calls=%async_computation | async-start | bytes 786432 | tf_op jit(solution)/shard_map/all_to_all | solution.py:64
  30.4 14.3 %all-to-all-start.1 = ((bf16[16,2,3,2048]{3,1,2,0:T(2,128)(2,1)}), bf16[16,2,3,2048]{3,1,2,0:T(2,128)(2,1)S(1)}, u32[]{:S(2)}, u32[]{:S(2)}) async-start(bf16[16,2,3,2048]{3,1,2,0:T(2,128)(2,1)} %broadcast_select_fusion.1), calls=%async_computation.1 | async-start | bytes 786432 | tf_op jit(solution)/shard_map/all_to_all | solution.py:70
  44.8 50.8 %all-to-all-start.2 = ((bf16[4,8,16,2048]{3,2,0,1:T(8,128)(2,1)}), bf16[4,8,16,2048]{3,2,0,1:T(8,128)(2,1)}, u32[]{:S(2)}, u32[]{:S(2)}) async-start(bf16[4,8,16,2048]{3,2,0,1:T(8,128)(2,1)} %copy.174), calls=%async_computation.2 | async-start | bytes 4194304 | tf_op jit(solution)/shard_map/all_to_all | solution.py:65
  95.5 97.6 %all-to-all-start.4 = ((bf16[4,4,256,512]{3,2,0,1:T(8,128)(2,1)}), bf16[4,4,256,512]{3,2,0,1:T(8,128)(2,1)}, u32[]{:S(2)}, u32[]{:S(2)}) async-start(bf16[4,4,256,512]{3,2,0,1:T(8,128)(2,1)} %copy.185), calls=%async_computation.4 | async-start | bytes 8388608 | tf_op jit(solution)/shard_map/all_to_all | solution.py:66
  193.1 97.6 %all-to-all-start.6 = ((bf16[4,4,256,512]{3,2,0,1:T(8,128)(2,1)}), bf16[4,4,256,512]{3,2,0,1:T(8,128)(2,1)}, u32[]{:S(2)}, u32[]{:S(2)}) async-start(bf16[4,4,256,512]{3,2,0,1:T(8,128)(2,1)} %copy.189), calls=%async_computation.6 | async-start | bytes 8388608 | tf_op jit(solution)/shard_map/all_to_all | solution.py:67
  204.7 90.4 %copy-start.15 = (s32[8,16]{1,0:T(8,128)S(1)}, s32[8,16]{1,0:T(8,128)}, u32[]{:S(2)}) copy-start(s32[8,16]{1,0:T(8,128)} %param.39) | copy-start | bytes 1540
  290.6 52.2 %all-to-all-start.3 = ((bf16[16,2,16,2048]{3,2,1,0:T(8,128)(2,1)}), bf16[16,2,16,2048]{3,2,1,0:T(8,128)(2,1)}, u32[]{:S(2)}, u32[]{:S(2)}) async-start(bf16[16,2,16,2048]{3,2,1,0:T(8,128)(2,1)} %broadcast_select_fusion), calls=%async_computation.3 | async-start | bytes 4194304 | tf_op jit(solution)/shard_map/all_to_all | solution.py:73
  342.9 97.6 %all-to-all-start.5 = ((bf16[16,1,256,512]{3,2,1,0:T(8,128)(2,1)}), bf16[16,1,256,512]{3,2,1,0:T(8,128)(2,1)}, u32[]{:S(2)}, u32[]{:S(2)}) async-start(bf16[16,1,256,512]{3,2,1,0:T(8,128)(2,1)} %get-tuple-element.29), calls=%async_computation.5 | async-start | bytes 8388608 | tf_op jit(solution)/shard_map/all_to_all | solution.py:76
  440.4 5.3 copy-start.17
  440.4 6.2 %copy-start.6 = (bf16[4,4,4096]{2,1,0:T(4,128)(2,1)S(1)}, bf16[4,4,4096]{2,1,0:T(4,128)(2,1)}, u32[]{:S(2)}) copy-start(bf16[4,4,4096]{2,1,0:T(4,128)(2,1)} %param.33) | copy-start | bytes 393220
  440.4 6.3 %copy-start.11 = (bf16[4,4,512]{2,1,0:T(4,128)(2,1)S(1)}, bf16[4,4,512]{2,1,0:T(4,128)(2,1)}, u32[]{:S(2)}) copy-start(bf16[4,4,512]{2,1,0:T(4,128)(2,1)} %param.34) | copy-start | bytes 49156
  440.5 6.4 %copy-start.12 = (bf16[4,4,512]{2,1,0:T(4,128)(2,1)S(1)}, bf16[4,4,512]{2,1,0:T(4,128)(2,1)}, u32[]{:S(2)}) copy-start(bf16[4,4,512]{2,1,0:T(4,128)(2,1)} %param.35) | copy-start | bytes 49156
  440.5 7.0 %copy-start.7 = (bf16[4,8,2048]{2,1,0:T(8,128)(2,1)S(1)}, bf16[4,8,2048]{2,1,0:T(8,128)(2,1)}, u32[]{:S(2)}) copy-start(bf16[4,8,2048]{2,1,0:T(8,128)(2,1)} %param.21) | copy-start | bytes 393220
  440.5 7.1 %copy-start.13 = (bf16[4,2048]{1,0:T(4,128)(2,1)S(1)}, bf16[4,2048]{1,0:T(4,128)(2,1)}, u32[]{:S(2)}) copy-start(bf16[4,2048]{1,0:T(4,128)(2,1)} %param.25) | copy-start | bytes 49156
  440.5 7.1 %copy-start.8 = (f32[16,2048]{1,0:T(8,128)S(1)}, f32[16,2048]{1,0:T(8,128)}, u32[]{:S(2)}) copy-start(f32[16,2048]{1,0:T(8,128)} %param.31) | copy-start | bytes 393220
  440.5 97.7 %all-to-all-start.7 = ((bf16[16,1,256,512]{3,2,1,0:T(8,128)(2,1)}), bf16[16,1,256,512]{3,2,1,0:T(8,128)(2,1)}, u32[]{:S(2)}, u32[]{:S(2)}) async-start(bf16[16,1,256,512]{3,2,1,0:T(8,128)(2,1)} %get-tuple-element.30), calls=%async_computation.7 | async-start | bytes 8388608 | tf_op jit(solution)/shard_map/all_to_all | solution.py:79
  445.5 3.7 copy-start.9
  445.5 36.4 %all-reduce.2.cloned.1.call-start = ((), (), s32[]{:S(2)}) async-start(), calls=%async_computation.8 | async-start | bytes 163840 | tf_op jit(solution)/shard_map/psum | solution.py:126
  446.8 2.0 copy-start.2
  447.5 35.4 %copy-start.16 = (f32[512]{0:T(512)S(1)}, f32[512]{0:T(512)}, u32[]{:S(2)}) copy-start(f32[512]{0:T(512)} %param.28) | copy-start | bytes 6148
  496.7 1.0 copy-start.1
  496.7 1.0 copy-start.4
  496.7 1.0 copy-start.14
  500.7 7.3 %copy-start.3 = (bf16[4,4,4,8,128]{4,3,2,1,0:T(8,128)(2,1)S(1)}, bf16[4,4,4,8,128]{4,3,2,1,0:T(8,128)(2,1)}, u32[]{:S(2)}) copy-start(bf16[4,4,4,8,128]{4,3,2,1,0:T(8,128)(2,1)} %copy-done.2) | copy-start | bytes 393220
  508.0 2.9 copy-start.5
  538.2 7.3 %copy-start.10 = (f32[4,4,4,128]{3,2,1,0:T(4,128)S(1)}, f32[4,4,4,128]{3,2,1,0:T(4,128)}, u32[]{:S(2)}) copy-start(f32[4,4,4,128]{3,2,1,0:T(4,128)} %reshape.155) | copy-start | bytes 98308
Sparse Core Ops, SparseCore 0:
  451.0 30.8 all-reduce.1
where the time goes:
time: 558 us; the launch traced here: 556 us
  waiting for transfers between devices  409 us (73%)
  local copies, waits for them, and re-layouts  58.7 us (11%)
  starting transfers between devices  38.6 us (7%)
  other arithmetic  25.3 us (5%)
  between operations  14.4 us (3%)
  matrix products  10.7 us (2%)
    all_to_all x1, waiting for transfers between devices, body(): lax.all_to_all(choose_rows(arrived[2], cache_picks), 'dp', split_axis=0,...  92.5 us
    all_to_all x1, waiting for transfers between devices, body(): lax.all_to_all(key_cache, 'dp', split_axis=1, concat_axis=0, tiled=True)  88.1 us
    all_to_all x1, waiting for transfers between devices, body(): lax.all_to_all(value_cache, 'dp', split_axis=1, concat_axis=0, tiled=True)  82.8 us
    all_to_all x1, waiting for transfers between devices, body(): lax.all_to_all(scan_state, 'dp', split_axis=1, concat_axis=0, tiled=True)  41.7 us
    all_to_all x1, waiting for transfers between devices, body(): lax.all_to_all(choose_rows(arrived[1], state_picks), 'dp', split_axis=0,...  30.2 us
    psum x1, waiting for transfers between devices, body(): projected = lax.psum(partial_sums, ('tensor', 'sub'))  28.8 us
    all_to_all x1, waiting for transfers between devices, body(): lax.all_to_all(choose_rows(arrived[3], cache_picks), 'dp', split_axis=0,...  26.9 us
    unnamed x43, local copies, waits for them, and re-layouts  16.2 us
  transfers between devices with their start and end apart: 9, of which 9 were waited for; matrix products, arithmetic and copies ran while one was open for 14% of the time, Pallas kernels for 0%

commit v1 on v0

--- a/solution.py
+++ b/solution.py
@@ -1,14 +1,621 @@
+import functools
+
 import jax
 import jax.numpy as jnp
+import numpy as np
 from jax import lax
+from jax.experimental import pallas as pl
+from jax.experimental.pallas import tpu as pltpu
 from jax.sharding import PartitionSpec as P
 
 HEADS = 64
 KV_HEADS = 8
 HEAD_DIM = 128
-
+GROUP = HEADS // KV_HEADS
 
 big_negative = -1e30
+
+TIERS = ((16, 12, 12), (18, 13, 13), (20, 15, 15), (24, 18, 18), (32, 32, 32))
+VMEM = 48 * 1024 * 1024
+TINY = pl.CostEstimate(flops=1000, bytes_accessed=1000, transcendentals=0)
+
+
+def pairs(mask):
+    return [(i, i ^ mask) for i in range(4)]
+
+
+def send(x, mask):
+    return lax.ppermute(x, "dp", pairs(mask))
+
+
+def plan_kernel(me_ref, parents_ref, plan):
+    me = me_ref[0]
+    row = lax.broadcasted_iota(jnp.int32, (128, 1), 0)
+    owner = row // 32
+    child_owner = lax.broadcasted_iota(jnp.int32, (128, 16), 1) // 4
+    prompt = lax.broadcasted_iota(jnp.int32, (128, 8), 1)
+    spread = jnp.where(lax.broadcasted_iota(jnp.int32, (128, 8), 0) % 8 == prompt, 1.0, 0.0)
+    tiled = jnp.dot(
+        spread, parents_ref[...].astype(jnp.float32), preferred_element_type=jnp.float32
+    ).astype(jnp.int32)
+    equal = tiled == row // 8
+    child_lane = lax.broadcasted_iota(jnp.int32, (128, 16), 1)
+    chosen = child_lane == me * 4 + row // 8
+    target = jnp.sum(jnp.where(chosen, tiled, 0), axis=1, keepdims=True) * 8 + row % 8
+
+    def wanted(mask):
+        hit = equal & (child_owner == (owner ^ mask))
+        return jnp.max(jnp.where(hit, 1.0, 0.0), axis=1, keepdims=True)
+
+    passed = wanted(3)
+    crossing = wanted(2) * (1.0 - passed)
+    beside = wanted(1)
+    lane = lax.broadcasted_iota(jnp.int32, (128, 128), 1)
+    down = lax.broadcasted_iota(jnp.int32, (128, 128), 0)
+    flags = jnp.where(
+        lane == 0, passed, jnp.where(lane == 1, crossing, jnp.where(lane == 2, beside, 0.0))
+    )
+    same = lane // 32 == down // 32
+    before = jnp.where(same & (lane < down), 1.0, 0.0)
+    ahead = jnp.dot(before, flags, preferred_element_type=jnp.float32)
+    totals = jnp.dot(jnp.where(same, 1.0, 0.0), flags, preferred_element_type=jnp.float32)
+    x_slot = jnp.where(
+        passed > 0.0,
+        ahead[:, 0:1],
+        jnp.where(crossing > 0.0, totals[:, 0:1] + ahead[:, 1:2], -1.0),
+    ).astype(jnp.int32)
+    o_slot = jnp.where(beside > 0.0, ahead[:, 2:3], -1.0).astype(jnp.int32)
+    mine = owner == me
+    local = row % 32
+
+    def listing(slot_of):
+        hit = (slot_of == lane) & mine
+        return jnp.max(jnp.where(hit, local, -1), axis=0, keepdims=True)
+
+    place = jnp.where(
+        mine,
+        local,
+        jnp.where(
+            owner == (me ^ 2),
+            32 + x_slot,
+            jnp.where(owner == (me ^ 1), 64 + o_slot, 96 + x_slot),
+        ),
+    )
+    place_across = jnp.sum(jnp.where(lane == down, place, 0), axis=0, keepdims=True)
+    code_down = jnp.sum(jnp.where(lane == target, place_across, 0), axis=1, keepdims=True)
+    code = jnp.sum(jnp.where(lane == down, code_down, 0), axis=0, keepdims=True)
+    x_most = jnp.max(totals[:, 0:1] + totals[:, 1:2], axis=0, keepdims=True)
+    f_most = jnp.max(totals[:, 0:1], axis=0, keepdims=True)
+    o_most = jnp.max(totals[:, 2:3], axis=0, keepdims=True)
+    tier = jnp.zeros((1, 1), jnp.int32)
+    for c, f, o in TIERS[:-1]:
+        over = (x_most > float(c)) | (f_most > float(f)) | (o_most > float(o))
+        tier += jnp.where(over, 1, 0)
+    handed = jnp.full((1, 1), TIERS[-1][1], jnp.int32)
+    for index in range(len(TIERS) - 1):
+        handed = jnp.where(tier == index, TIERS[index][1], handed)
+    child = row < 32
+    late = child & ((code_down >= 96) | ((code_down >= 32 + handed) & (code_down < 64)))
+    early = child & jnp.logical_not(late)
+    groups = jnp.where(
+        lane == 0, jnp.where(early, 1.0, 0.0), jnp.where(lane == 1, jnp.where(late, 1.0, 0.0), 0.0)
+    )
+    earlier = jnp.where(lane < down, 1.0, 0.0)
+    position = jnp.dot(earlier, groups, preferred_element_type=jnp.float32).astype(jnp.int32)
+    amount = jnp.sum(groups, axis=0, keepdims=True).astype(jnp.int32)
+
+    def members(index, group):
+        hit = (position[:, index : index + 1] == lane) & group
+        return jnp.max(jnp.where(hit, row, -1), axis=0, keepdims=True)
+
+    plan[0:1, :] = listing(x_slot)
+    plan[1:2, :] = listing(o_slot)
+    plan[2:3, :] = code
+    plan[3:4, :] = jnp.broadcast_to(tier, (1, 128))
+    plan[4:5, :] = members(0, early)
+    plan[5:6, :] = members(1, late)
+    plan[6:7, :] = amount
+    plan[7:8, :] = jnp.zeros((1, 128), jnp.int32)
+
+
+def make_plan(parents, me):
+    return pl.pallas_call(
+        plan_kernel,
+        in_specs=[pl.BlockSpec(memory_space=pltpu.SMEM), pl.BlockSpec(memory_space=pltpu.VMEM)],
+        out_specs=pl.BlockSpec(memory_space=pltpu.VMEM),
+        out_shape=jax.ShapeDtypeStruct((8, 128), jnp.int32),
+        name="plan",
+    )(me.reshape(1), parents)
+
+
+def attend_kernel(heads, q_ref, k_ref, v_ref, lo_ref, hi_ref, *outs):
+    lo = jnp.concatenate([lo_ref[0]] * GROUP, axis=0)
+    hi = jnp.concatenate([hi_ref[0]] * GROUP, axis=0)
+    beams, _, length, _ = k_ref.shape
+    keys = beams * length
+    column = lax.broadcasted_iota(jnp.int32, (16 * GROUP, keys), 1)
+    live = (column >= lo) & (column < hi)
+    local = (hi > lo).astype(jnp.float32)
+    scale = HEAD_DIM**-0.5
+    width = GROUP * HEAD_DIM
+    key_base = heads * width
+    value_base = key_base + heads * HEAD_DIM
+    for k in range(heads):
+        q = jnp.concatenate(
+            [
+                q_ref[0, :, k * width + g * HEAD_DIM : k * width + (g + 1) * HEAD_DIM]
+                for g in range(GROUP)
+            ],
+            axis=0,
+        )
+        head = slice(k * HEAD_DIM, (k + 1) * HEAD_DIM)
+        keys_here = k_ref[:, 0, :, head].reshape(keys, HEAD_DIM)
+        values_here = v_ref[:, 0, :, head].reshape(keys, HEAD_DIM)
+        new_key = q_ref[0, :, key_base + k * HEAD_DIM : key_base + (k + 1) * HEAD_DIM]
+        new_value = q_ref[0, :, value_base + k * HEAD_DIM : value_base + (k + 1) * HEAD_DIM]
+        scores = (
+            lax.dot_general(
+                q, keys_here, (((1,), (1,)), ((), ())), preferred_element_type=jnp.float32
+            )
+            * scale
+        )
+        new_keys = jnp.concatenate([new_key.astype(jnp.float32)] * GROUP, axis=0)
+        new_values = jnp.concatenate([new_value.astype(jnp.float32)] * GROUP, axis=0)
+        fresh = jnp.sum(q.astype(jnp.float32) * new_keys, axis=1, keepdims=True) * scale
+        scores = jnp.where(live, scores, big_negative)
+        top = jnp.maximum(jnp.max(scores, axis=1, keepdims=True), fresh)
+        weights = jnp.exp(scores - top)
+        fresh_weight = jnp.exp(fresh - top)
+        share = 1.0 / (jnp.sum(weights, axis=1, keepdims=True) + fresh_weight)
+        half = (weights * share).astype(jnp.bfloat16)
+        fresh_half = (fresh_weight * share).astype(jnp.bfloat16).astype(jnp.float32)
+        mixed = jnp.dot(half, values_here, preferred_element_type=jnp.float32)
+        mixed = jnp.where(local > 0.0, mixed + fresh_half * new_values, 0.0).astype(jnp.bfloat16)
+        for block in range(4):
+            out = outs[block % 2]
+            for g in range(GROUP):
+                out[block // 2, 0, :, k * width + g * HEAD_DIM : k * width + (g + 1) * HEAD_DIM] = mixed[
+                    g * 16 + 4 * block : g * 16 + 4 * block + 4
+                ]
+
+
+def attend(queries, keys, values, lo, hi):
+    prompts, children, width = queries.shape
+    beams, _, length, depth = keys.shape
+    heads = depth // HEAD_DIM
+    wide = heads * GROUP * HEAD_DIM
+    spec = pl.BlockSpec((beams, 1, length, depth), lambda p: (0, p, 0, 0))
+    bound = pl.BlockSpec((1, children, 1), lambda p: (p, 0, 0))
+    return pl.pallas_call(
+        functools.partial(attend_kernel, heads),
+        grid=(prompts,),
+        in_specs=[pl.BlockSpec((1, children, width), lambda p: (p, 0, 0)), spec, spec, bound, bound],
+        out_specs=[pl.BlockSpec((2, 1, 4, wide), lambda p: (0, p, 0, 0))] * 2,
+        out_shape=[jax.ShapeDtypeStruct((2, prompts, 4, wide), jnp.bfloat16)] * 2,
+        compiler_params=pltpu.CompilerParams(vmem_limit_bytes=VMEM),
+        cost_estimate=TINY,
+        name="attend",
+    )(queries, keys, values, lo, hi)
+
+
+def one_hot(column, width):
+    lane = lax.broadcasted_iota(jnp.int32, (column.shape[0], width), 1)
+    return (lane == column).astype(jnp.bfloat16)
+
+
+def pick(column, table):
+    return jnp.dot(one_hot(column, table.shape[0]), table, preferred_element_type=jnp.float32)
+
+
+def pack_taps_kernel(*refs):
+    half = len(refs) // 2
+    taps = refs[half][...]
+    for column, out in zip(refs[:half], refs[half + 1 :]):
+        out[...] = pick(column[...], taps).astype(jnp.bfloat16)
+
+
+def pack_taps(tier, plan, taps):
+    c, f, o = tier
+    width = taps.shape[1]
+    listings = [plan[0, :c], plan[1, :o]] + ([plan[0, :f]] if c > f else [])
+    columns = [
+        jnp.concatenate([jnp.where(base >= 0, base + 32 * k, -1) for k in range(3)])[:, None]
+        for base in listings
+    ]
+    vmem = pl.BlockSpec(memory_space=pltpu.VMEM)
+    outs = pl.pallas_call(
+        pack_taps_kernel,
+        in_specs=[vmem] * (len(columns) + 1),
+        out_specs=[vmem] * len(columns),
+        out_shape=[jax.ShapeDtypeStruct((x.shape[0], width), jnp.bfloat16) for x in columns],
+        compiler_params=pltpu.CompilerParams(vmem_limit_bytes=VMEM),
+        cost_estimate=TINY,
+        name="pack_taps",
+    )(*columns, taps)
+    return outs if c > f else (*outs, outs[0])
+
+
+def pack_kernel(tier, plan, state, *rest):
+    c, f, o = tier
+    sems = rest[-1]
+    xa, out = rest[0], rest[-2]
+
+    def copies(which, first, count, target, base):
+        def start(s, _):
+            row = jnp.maximum(plan[which, first + s], 0)
+            pltpu.make_async_copy(state.at[row], target.at[s], sems.at[base + s]).start()
+            return 0
+
+        lax.fori_loop(0, count, start, 0)
+
+    copies(0, 0, f, xa, 0)
+    copies(1, 0, o, out, c)
+    if c > f:
+        copies(0, f, c - f, rest[1], f)
+
+    def finish(s, _):
+        pltpu.make_async_copy(state.at[0], xa.at[0], sems.at[s]).wait()
+        return 0
+
+    lax.fori_loop(0, c + o, finish, 0)
+
+
+def pack(tier, plan, state):
+    c, f, o = tier
+    rows = [f] + ([c - f] if c > f else []) + [o]
+    vmem = pl.BlockSpec(memory_space=pltpu.VMEM)
+    anywhere = pl.BlockSpec(memory_space=pl.ANY)
+    outs = pl.pallas_call(
+        functools.partial(pack_kernel, tier),
+        in_specs=[pl.BlockSpec(memory_space=pltpu.SMEM), vmem],
+        out_specs=[anywhere] * len(rows),
+        out_shape=[jax.ShapeDtypeStruct((n,) + state.shape[1:], jnp.bfloat16) for n in rows],
+        scratch_shapes=[pltpu.SemaphoreType.DMA((c + o,))],
+        compiler_params=pltpu.CompilerParams(vmem_limit_bytes=VMEM),
+        cost_estimate=TINY,
+        name="pack",
+    )(plan, state)
+    if c == f:
+        return outs[0], None, outs[1]
+    return outs
+
+
+def conv_kernel(code, token, weight, bias, select, taps, *rest):
+    *tables, conv_out, next_taps, partial = rest
+    count = token.shape[0]
+    code = code[...]
+    tap = lax.broadcasted_iota(jnp.int32, (3 * count, 1), 0) // count
+
+    def part(base, table):
+        size = table.shape[0] // 3
+        slot = code - base
+        inside = (slot >= 0) & (slot < size)
+        return pick(jnp.where(inside, slot + tap * size, -1), table[...])
+
+    window = part(0, taps)
+    for index, table in enumerate(tables):
+        window += part(32 * (index + 1), table)
+    fresh = token[...]
+    next_taps[0 : 2 * count, :] = window[count:].astype(jnp.bfloat16)
+    next_taps[2 * count :, :] = fresh
+    w = weight[...].astype(jnp.float32)
+    total = window[:count] * w[0:1]
+    total += window[count : 2 * count] * w[1:2]
+    total += window[2 * count :] * w[2:3]
+    total += fresh.astype(jnp.float32) * w[3:4]
+    v = total + bias[...]
+    conv = v / (1.0 + jnp.exp(-v))
+    conv_out[...] = conv
+    partial[...] = jnp.dot(
+        conv.astype(jnp.bfloat16), select[...], preferred_element_type=jnp.float32
+    )
+
+
+def convolve(code, token, weight, bias, select, taps, tables):
+    count, width = token.shape
+    vmem = pl.BlockSpec(memory_space=pltpu.VMEM)
+    return pl.pallas_call(
+        conv_kernel,
+        in_specs=[vmem] * (6 + len(tables)),
+        out_specs=[vmem] * 3,
+        out_shape=[
+            jax.ShapeDtypeStruct((count, width), jnp.float32),
+            jax.ShapeDtypeStruct((3 * count, width), jnp.bfloat16),
+            jax.ShapeDtypeStruct((count, select.shape[1]), jnp.float32),
+        ],
+        compiler_params=pltpu.CompilerParams(vmem_limit_bytes=VMEM),
+        cost_estimate=TINY,
+        name="convolve",
+    )(code, token, weight, bias, select, taps, *tables)
+
+
+def step_kernel(projected, across, gain, weight, bias, step, b_wide, c_wide):
+    rank = gain.shape[1]
+    raw = projected[:, :rank]
+    mean = jnp.mean(raw * raw, axis=1, keepdims=True)
+    norm = (raw * lax.rsqrt(mean + 1e-06) * gain[...]).astype(jnp.bfloat16)
+    v = jnp.dot(norm, weight[...], preferred_element_type=jnp.float32) + bias[...]
+    step[...] = jnp.maximum(v, 0.0) + jnp.log1p(jnp.exp(-jnp.abs(v)))
+    states = b_wide.shape[1]
+    for r in range(b_wide.shape[0]):
+        b_wide[r] = jnp.broadcast_to(across[:states, r : r + 1], b_wide.shape[1:])
+        c_wide[r] = jnp.broadcast_to(across[states:, r : r + 1], c_wide.shape[1:])
+
+
+def step_sizes(projected, gain, weight, bias):
+    count, width = projected.shape[0], weight.shape[1]
+    rank = gain.shape[1]
+    across = projected[:, rank:].T
+    states = across.shape[0] // 2
+    vmem = pl.BlockSpec(memory_space=pltpu.VMEM)
+    wide = jax.ShapeDtypeStruct((count, states, 128), jnp.float32)
+    return pl.pallas_call(
+        step_kernel,
+        in_specs=[vmem] * 5,
+        out_specs=[vmem] * 3,
+        out_shape=[jax.ShapeDtypeStruct((count, width), jnp.float32), wide, wide],
+        compiler_params=pltpu.CompilerParams(vmem_limit_bytes=VMEM),
+        cost_estimate=TINY,
+        name="step_sizes",
+    )(projected, across, gain, weight, bias)
+
+
+def advance(plan, which, starts, step, conv, rates, b_in, c_in, held, done, lines, next_state, sems):
+    total = plan[6, which]
+    in_sems, out_sems = sems
+
+    def begin(n, _):
+        r = plan[4 + which, n]
+        where = plan[2, r]
+        for condition, source, base in starts:
+
+            @pl.when(condition(where))
+            def _(source=source, base=base):
+                pltpu.make_async_copy(source.at[where - base], held.at[n], in_sems.at[n]).start()
+
+        return 0
+
+    lax.fori_loop(0, total, begin, 0)
+    def work(n, _):
+        r = plan[4 + which, n]
+        pltpu.make_async_copy(next_state.at[0], held.at[n], in_sems.at[n]).wait()
+        b = b_in[r]
+        c_out = c_in[r]
+        sizes = step[pl.ds(r, 1), :]
+        gains = sizes * conv[pl.ds(r, 1), :]
+        readouts = []
+        for first in range(0, step.shape[1], 128):
+            part = slice(first, first + 128)
+            state = held[n, :, part].astype(jnp.float32)
+            new = jnp.exp(-sizes[:, part] * rates[:, part]) * state + gains[:, part] * b
+            done[n, :, part] = new.astype(jnp.bfloat16)
+            readouts.append(jnp.sum(c_out * new, axis=0, keepdims=True))
+        lines[pl.ds(r, 1), :] = lines[pl.ds(r, 1), :] + jnp.concatenate(readouts, axis=1)
+        pltpu.make_async_copy(done.at[n], next_state.at[r], out_sems.at[n]).start()
+        return 0
+
+    lax.fori_loop(0, total, work, 0)
+
+    def finish(n, _):
+        pltpu.make_async_copy(done.at[n], next_state.at[0], out_sems.at[n]).wait()
+        return 0
+
+    lax.fori_loop(0, total, finish, 0)
+
+
+def early_kernel(
+    tier, plan, step, conv, decay_log, skip, gate, b_in, c_in, local, xa, beside, next_state, lines, opened, held, done, rates, *sems
+):
+    f = tier[1]
+    rates[...] = jnp.exp(decay_log[...])
+    lines[...] = skip[...] * conv[...]
+    gates = gate[...].astype(jnp.float32)
+    opened[...] = gates / (1.0 + jnp.exp(-gates))
+    starts = (
+        (lambda w: w < 32, local, 0),
+        (lambda w: (w >= 32) & (w < 32 + f), xa, 32),
+        (lambda w: (w >= 64) & (w < 96), beside, 64),
+    )
+    advance(plan, 0, starts, step, conv, rates, b_in, c_in, held, done, lines, next_state, sems)
+
+
+def late_kernel(
+    tier, has_xb, plan, step, conv, decay_log, b_in, c_in, lines_in, opened, *rest
+):
+    f = tier[1]
+    sources, rest = rest[: 2 if has_xb else 1], rest[2 if has_xb else 1 :]
+    _, next_state, output, held, done, rates, lines, *sems = rest
+    rates[...] = jnp.exp(decay_log[...])
+    lines[...] = lines_in[...]
+    starts = [(lambda w: w >= 96, sources[-1], 96)]
+    if has_xb:
+        starts.append((lambda w: w < 96, sources[0], 32 + f))
+    advance(plan, 1, starts, step, conv, rates, b_in, c_in, held, done, lines, next_state, sems)
+    output[...] = (lines[...] * opened[...]).astype(jnp.bfloat16)
+
+
+def scan_scratch(count, states, width):
+    return [
+        pltpu.VMEM((count, states, width), jnp.bfloat16),
+        pltpu.VMEM((count, states, width), jnp.bfloat16),
+        pltpu.VMEM((states, width), jnp.float32),
+    ], [pltpu.SemaphoreType.DMA((count,)), pltpu.SemaphoreType.DMA((count,))]
+
+
+def early(tier, plan, step, conv, decay_log, skip, gate, b_in, c_in, local, xa, beside):
+    count, width = step.shape
+    states = decay_log.shape[0]
+    vmem = pl.BlockSpec(memory_space=pltpu.VMEM)
+    anywhere = pl.BlockSpec(memory_space=pl.ANY)
+    arrays, sems = scan_scratch(count, states, width)
+    return pl.pallas_call(
+        functools.partial(early_kernel, tier),
+        in_specs=[pl.BlockSpec(memory_space=pltpu.SMEM)] + [vmem] * 7 + [anywhere] * 3,
+        out_specs=[anywhere, vmem, vmem],
+        out_shape=[
+            jax.ShapeDtypeStruct((count, states, width), jnp.bfloat16),
+            jax.ShapeDtypeStruct((count, width), jnp.float32),
+            jax.ShapeDtypeStruct((count, width), jnp.float32),
+        ],
+        scratch_shapes=arrays + sems,
+        compiler_params=pltpu.CompilerParams(vmem_limit_bytes=VMEM),
+        cost_estimate=TINY,
+        name="early",
+    )(plan, step, conv, decay_log, skip, gate, b_in, c_in, local, xa, beside)
+
+
+def late(tier, plan, step, conv, decay_log, b_in, c_in, lines, opened, buffers, next_state):
+    count, width = step.shape
+    states = decay_log.shape[0]
+    vmem = pl.BlockSpec(memory_space=pltpu.VMEM)
+    anywhere = pl.BlockSpec(memory_space=pl.ANY)
+    arrays, sems = scan_scratch(count, states, width)
+    return pl.pallas_call(
+        functools.partial(late_kernel, tier, len(buffers) == 2),
+        in_specs=[pl.BlockSpec(memory_space=pltpu.SMEM)]
+        + [vmem] * 7
+        + [anywhere] * (len(buffers) + 1),
+        out_specs=[anywhere, vmem],
+        out_shape=[
+            jax.ShapeDtypeStruct((count, states, width), jnp.bfloat16),
+            jax.ShapeDtypeStruct((count, width), jnp.bfloat16),
+        ],
+        scratch_shapes=arrays + [pltpu.VMEM((count, width), jnp.float32)] + sems,
+        input_output_aliases={8 + len(buffers): 0},
+        compiler_params=pltpu.CompilerParams(vmem_limit_bytes=VMEM),
+        cost_estimate=TINY,
+        name="late",
+    )(plan, step, conv, decay_log, b_in, c_in, lines, opened, *buffers, next_state)
+
+
+def swap(x, axis):
+    size = lax.axis_size(axis)
+    return x + lax.ppermute(x, axis, [(i, i ^ 1) for i in range(size)])
+
+
+def quick_body(
+    token_input,
+    gate_input,
+    conv_taps,
+    scan_state,
+    conv_weight,
+    conv_bias,
+    select_weight,
+    step_gain,
+    step_weight,
+    step_bias,
+    decay_log,
+    skip_gain,
+    query,
+    fresh_key,
+    fresh_value,
+    key_cache,
+    value_cache,
+    cache_lengths,
+    parents,
+):
+    me = lax.axis_index("dp")
+    beams, prompts, width = token_input.shape
+    states, rank = decay_log.shape[0], step_gain.shape[0]
+    count = beams * prompts
+    cache_prompts, length = key_cache.shape[1], key_cache.shape[2]
+    first = lax.axis_index("sub") * cache_prompts
+
+    fresh = jnp.concatenate([fresh_key, fresh_value], axis=2)
+    asked = [query, send(query, 1), send(query, 2)]
+    fresh = [fresh, send(fresh, 1), send(fresh, 2)]
+
+    plan = make_plan(parents, me)
+    here = lax.dynamic_slice_in_dim(parents, first, cache_prompts, 0)
+    lengths = lax.dynamic_slice_in_dim(cache_lengths, first, cache_prompts, 1)
+    related = jnp.concatenate(
+        [lax.dynamic_slice_in_dim(here, (me ^ mask) * beams, beams, 1) for mask in range(4)], axis=1
+    )
+    live = jnp.sum(
+        jnp.where(related[:, :, None] == np.arange(16)[None, None, :], lengths.T[:, None, :], 0), axis=2
+    )
+    local = related // beams == me
+    lo = jnp.where(local, (related % beams) * length, 0)
+    hi = jnp.where(local, lo + live, 0)
+    lo, hi = lo[:, :, None], hi[:, :, None]
+    taps = conv_taps.transpose(2, 0, 1, 3).reshape(3 * count, width)
+    state = scan_state.reshape(count, states, width)
+    code_column = jnp.tile(plan[2, :count], 3)[:, None]
+
+    def run(limits):
+        c, f, o = limits
+
+        def branch(plan, code_column, taps, state, asked, fresh, lo, hi):
+            asked = [*asked, send(asked[2], 1)]
+            fresh = [*fresh, send(fresh[2], 1)]
+            tx, to, tf = pack_taps(limits, plan, taps)
+            tables = [send(tx, 2), send(to, 1), send(tf, 3)]
+            xa, xb, near = pack(limits, plan, state)
+            xa, near, *tables = lax.optimization_barrier((xa, near, *tables))
+            xa, near = send(xa, 2), send(near, 1)
+            conv, next_taps, partial = convolve(
+                code_column,
+                token_input.reshape(count, width),
+                conv_weight,
+                conv_bias[None],
+                select_weight,
+                taps,
+                tables,
+            )
+            partial = swap(partial, "sub")
+            asked = jnp.concatenate(asked, axis=0)
+            fresh = jnp.concatenate(fresh, axis=0)
+            queries = jnp.concatenate([asked, fresh], axis=2).transpose(1, 0, 2)
+            queries, partial = lax.optimization_barrier((queries, partial))
+            projected = swap(partial, "tensor")
+            outs = attend(queries, key_cache, value_cache, lo, hi)
+            step, b_in, c_in = step_sizes(projected, step_gain[None], step_weight, step_bias[None])
+            second = [*outs] if xb is None else [*outs, xb]
+            xa, near, step, *second = lax.optimization_barrier((xa, near, step, *second))
+            passed = send(xa, 1)
+            buffers = [passed] if xb is None else [send(second[2], 2), passed]
+            back = second[0] + send(second[1], 1)
+            attention = (back[0] + send(back[1], 2)).transpose(1, 0, 2)
+            next_state, lines, opened = early(
+                limits,
+                plan,
+                step,
+                conv,
+                decay_log,
+                skip_gain[None],
+                gate_input.reshape(count, width),
+                b_in,
+                c_in,
+                state,
+                xa,
+                near,
+            )
+            next_state, output = late(
+                limits, plan, step, conv, decay_log, b_in, c_in, lines, opened, buffers, next_state
+            )
+            next_taps = next_taps.reshape(3, beams, prompts, width).transpose(1, 2, 0, 3)
+            return next_state, next_taps, output, attention
+
+        return branch
+
+    next_state, next_taps, output, attention = lax.switch(
+        plan[3, 0],
+        [run(limits) for limits in TIERS],
+        plan,
+        code_column,
+        taps,
+        state,
+        asked,
+        fresh,
+        lo,
+        hi,
+    )
+    return (
+        next_state.reshape(beams, prompts, states, width),
+        next_taps,
+        output.reshape(beams, prompts, width),
+        attention,
+    )
 
 
 def choose_rows(array, picks):
@@ -20,7 +627,7 @@
     return lax.dynamic_slice_in_dim(parents, first, count, 0).T
 
 
-def body(
+def general_body(
     token_input,
     gate_input,
     conv_taps,
@@ -148,6 +755,15 @@
     return (state_next.astype(jnp.bfloat16), window[:, :, 1:, :], mamba_output, attention_output)
 
 
+def body(*arrays):
+    token_input, parents = arrays[0], arrays[-1]
+    sizes = (lax.axis_size("dp"), token_input.shape[0], token_input.shape[1], parents.shape[1])
+    paired = lax.axis_size("tensor") == 2 and lax.axis_size("sub") == 2
+    if sizes == (4, 4, 8, 16) and paired:
+        return quick_body(*arrays)
+    return general_body(*arrays)
+
+
 def solution(mesh):
     placed = (
         P("dp", "groups", ("tensor", "sub")),

time: 558 us -> 142 us (0.25)
  the two profiles are of different devices: /device:TPU:0 before, /device:TPU:6 now
where the time goes in v1:
time: 142 us; the launch traced here: 140 us
  waiting for transfers between devices  59.5 us (42%)
  Pallas kernels  33.2 us (23%)
  local copies, waits for them, and re-layouts  21.9 us (15%)
  starting transfers between devices  17.1 us (12%)
  other arithmetic  6.13 us (4%)
    ppermute x15, waiting for transfers between devices, send(): return lax.ppermute(x, 'dp', pairs(mask))  59.5 us
    ppermute x15, starting transfers between devices, send(): return lax.ppermute(x, 'dp', pairs(mask))  16.5 us
    pallas_call x1, Pallas kernels, attend(): pl.pallas_call(functools.partial(attend_kernel, heads), grid=(prompts,),...  9.72 us
    cond x54, local copies, waits for them, and re-layouts  8.52 us
    pallas_call x1, Pallas kernels, early(): pl.pallas_call(functools.partial(early_kernel, tier), in_specs=[pl.BlockS...  7.26 us
    another operation x5, local copies, waits for them, and re-layouts  5.54 us
    pallas_call x1, Pallas kernels, pack(): pl.pallas_call(functools.partial(pack_kernel, tier), in_specs=[pl.BlockSp...  5.47 us
    pallas_call x1, Pallas kernels, late(): pl.pallas_call(functools.partial(late_kernel, tier, len(buffers) == 2), i...  3.46 us
  transfers between devices with their start and end apart: 17, of which 5 were waited for; matrix products, arithmetic and copies ran while one was open for 12% of the time, Pallas kernels for 20%

profile of v1, /device:TPU:6, one launch (start us, length us, event | category | flops | bytes accessed | tf_op | source)
XLA Modules:
  0.0 139.8 jit_solution(10442535462803477210)
XLA Ops:
  2.1 2.7 %collective-permute-start.66 = (bf16[4,4,1024]{2,0,1:T(4,128)(2,1)S(1)}, bf16[4,4,1024]{2,0,1:T(4,128)(2,1)}, u32[]{:S(2)}, u32[]{:S(2)}) collective-permute-start(bf16[4,4,1024]{2,0,1:T(4,128)(2,1)S(1)} %copy_dynamic-update-slice_fusion), channel_id=1, source_target_pairs={{0,8},{4,12},{8,0},{12,4},{1,9},{5,13},{9,1},{13,5},{2,10},{6,14},... | collective-permute-start | bytes 98312 | tf_op jit(solution)/shard_map/ppermute | solution.py:28
  4.8 1.6 %collective-permute-start.67 = (bf16[4,4,1024]{2,0,1:T(4,128)(2,1)S(1)}, bf16[4,4,1024]{2,0,1:T(4,128)(2,1)}, u32[]{:S(2)}, u32[]{:S(2)}) collective-permute-start(bf16[4,4,1024]{2,0,1:T(4,128)(2,1)S(1)} %copy_dynamic-update-slice_fusion), channel_id=1, source_target_pairs={{0,4},{4,0},{8,12},{12,8},{1,5},{5,1},{9,13},{13,9},{2,6},{6,2},{1... | collective-permute-start | bytes 98312 | tf_op jit(solution)/shard_map/ppermute | solution.py:28
  6.3 1.0 copy.120
  9.8 1.8 %plan.1 = s32[8,128]{1,0:T(8,128)S(1)} custom-call(s32[1]{0:T(128)} %bitcast.118.me_ref, s32[8,16]{1,0:T(8,128)} %parents_ref.1), custom_call_target="tpu_custom_call" | custom-call | tf_op jit(solution)/shard_map/plan/pallas_call | solution.py:122
  12.8 3.0 %collective-permute-done.64 = bf16[4,4,4096]{2,0,1:T(4,128)(2,1)} collective-permute-done((bf16[4,4,4096]{2,0,1:T(4,128)(2,1)S(1)}, bf16[4,4,4096]{2,0,1:T(4,128)(2,1)}, u32[]{:S(2)}, u32[]{:S(2)}) %collective-permute-start.64) | collective-permute-done | bytes 131104 | tf_op jit(solution)/shard_map/ppermute | solution.py:28
  16.4 122.7 %conditional.1 = (bf16[32,16,2048]{2,1,0:T(8,128)(2,1)}, bf16[32,2048]{1,0:T(8,128)(2,1)}, bf16[4,8,3,2048]{3,1,2,0:T(8,128)(2,1)}, bf16[4,4,4096]{2,1,0:T(4,128)(2,1)}) conditional(s32[]{:T(128)} %bitcast.119, (s32[8,128]{1,0:T(8,128)S(1)}, bf16[4,8,16,2048]{3,2,1,0:T(8,128)(2,1)}, ...), branch_computations={%region_1.2_spmd, %region_2.3_spmd, %region_3.4_spmd, %region_4.5_... | conditional | flops 5485208 | bytes 66009580 | solution.py:601
  17.4 1.0 copy.163
  18.4 1.1 pack_taps.7
  20.1 1.1 collective-permute-start.27
  21.2 2.8 %collective-permute-start.28 = (bf16[45,2048]{1,0:T(8,128)(2,1)}, bf16[45,2048]{1,0:T(8,128)(2,1)}, u32[]{:S(2)}, u32[]{:S(2)}) collective-permute-start(bf16[45,2048]{1,0:T(8,128)(2,1)} %get-tuple-element.359), channel_id=1, source_target_pairs={{0,12},{4,8},{8,4},{12,0},{1,13},{5,9},{9,5},{13,1},{2,14},{6,10},... | collective-permute-start | bytes 552968 | tf_op jit(solution)/shard_map/cond/branch_2_fun/ppermute | solution.py:28
  23.9 2.0 %collective-permute-start.32 = (bf16[4,4,1024]{2,0,1:T(4,128)(2,1)}, bf16[4,4,1024]{2,0,1:T(4,128)(2,1)}, u32[]{:S(2)}, u32[]{:S(2)}) collective-permute-start(bf16[4,4,1024]{2,0,1:T(4,128)(2,1)} %get-tuple-element.367), channel_id=1, source_target_pairs={{0,4},{4,0},{8,12},{12,8},{1,5},{5,1},{9,13},{13,9},{2,6},{6,2},{1... | collective-permute-start | bytes 98312 | tf_op jit(solution)/shard_map/cond/branch_2_fun/ppermute | solution.py:28
  26.0 1.6 %select_reduce_fusion.2 = s32[4,16]{1,0:T(4,128)} fusion(s32[]{:T(128)} %get-tuple-element.849, s32[4,16,16]{2,1,0:T(8,128)} %copy-done.73, s32[4,16]{1,0:T(4,128)} %copy-done.99, s32[]{:T(128)} %get-tuple-element.886, s32[4,16]{1,0:T(4,128)} %copy-done.100), kind=kLoop, calls=%fused_computation.61 | loop fusion | flops 3008 | bytes 4872 | tf_op jit(solution)/shard_map/reduce_sum | solution.py:534
  27.5 5.5 %pack.7 = (bf16[15,16,2048]{2,1,0:T(8,128)(2,1)S(1)}, bf16[5,16,2048]{2,1,0:T(8,128)(2,1)S(1)}, bf16[15,16,2048]{2,1,0:T(8,128)(2,1)S(1)}) custom-call(s32[8,128]{1,0:T(8,128)S(1)} %get-tuple-element.841, bf16[32,16,2048]{2,1,0:T(8,128)(2,1)} %bitcast.353), custom_call_target="tpu_custom_call" | custom-call | flops 1000 | bytes 1000 | tf_op jit(solution)/shard_map/cond/branch_2_fun/pack/pallas_call | solution.py:268
  33.0 0.9 copy-done.33
  34.0 0.9 copy-done.34
  35.7 3.1 %copy.136.select = bf16[2048,544]{1,0:T(8,128)(2,1)S(1)} copy(bf16[2048,544]{0,1:T(8,128)(2,1)} %get-tuple-element.714) | data formatting | bytes 4456448 | tf_op jit(solution)/shard_map
  39.5 1.7 %copy.134 = bf16[4,4,4096]{2,0,1:T(4,128)(2,1)} copy(bf16[4,4,4096]{2,1,0:T(4,128)(2,1)} %get-tuple-element.705) | data formatting | bytes 262144 | tf_op jit(solution)/shard_map
  43.6 2.1 %convolve.7 = (f32[32,2048]{1,0:T(8,128)S(1)}, bf16[96,2048]{1,0:T(8,128)(2,1)S(1)}, f32[32,544]{1,0:T(8,128)S(1)}) custom-call(s32[96,1]{1,0:T(8,128)S(1)} %copy-done.22, bf16[32,2048]{1,0:T(8,128)(2,1)} %bitcast.371, bf16[4,2048]{1,0:T(4,128)(2,1)} %get-tuple-element.370.weight, f32[1,2048]{1,0:T(1,128)S(1)} %bitcast.376, ...), custom_call_target="tpu_custom_call" | custom-call | flops 1000 | bytes 1000 | tf_op jit(solution)/shard_map/cond/branch_2_fun/convolve/pallas_call | solution.py:317
  47.0 1.0 copy.106
  48.2 1.6 %collective-permute-start.30 = (bf16[15,16,2048]{2,1,0:T(8,128)(2,1)}, bf16[15,16,2048]{2,1,0:T(8,128)(2,1)S(1)}, u32[]{:S(2)}, u32[]{:S(2)}) collective-permute-start(bf16[15,16,2048]{2,1,0:T(8,128)(2,1)} %copy-done.33), channel_id=1, source_target_pairs={{0,4},{4,0},{8,12},{12,8},{1,5},{5,1},{9,13},{13,9},{2,6},{6,2},{1... | collective-permute-start | bytes 2949128 | tf_op jit(solution)/shard_map/cond/branch_2_fun/ppermute | solution.py:28
  49.8 1.6 %maximum_bitcast_fusion.2.q_ref = bf16[4,16,5120]{2,1,0:T(8,128)(2,1)S(1)} fusion(bf16[4,4,1024]{2,0,1:T(4,128)(2,1)} %collective-permute-done.32, bf16[4,4,1024]{2,0,1:T(4,128)(2,1)} %get-tuple-element.367, bf16[4,4,1024]{2,0,1:T(4,128)(2,1)} %get-tuple-element.366, bf16[4,4,1024]{2,0,1:T(4,128)(2,1)} %copy-done.78, ...), kind=kLoop, calls=%fused_computation.56 | loop fusion | flops 5242880 | bytes 1310720 | tf_op jit(solution)/shard_map/cond/branch_2_fun/transpose | solution.py:568
  52.9 9.7 %attend.7 = (bf16[2,4,4,4096]{3,2,1,0:T(4,128)(2,1)S(1)}, bf16[2,4,4,4096]{3,2,1,0:T(4,128)(2,1)S(1)}) custom-call(bf16[4,16,5120]{2,1,0:T(8,128)(2,1)S(1)} %maximum_bitcast_fusion.2.q_ref, bf16[4,4,256,512]{3,2,1,0:T(8,128)(2,1)} %get-tuple-element.383.k_ref, bf16[4,4,256,512]{3,2,1,0:T(8,128)(2,1)} %get-tuple-element.384.v_ref, ...), custom_call_target="tpu_custom_call" | custom-call | flops 1000 | bytes 1000 | tf_op jit(solution)/shard_map/cond/branch_2_fun/attend/pallas_call | solution.py:189
  62.7 1.2 add.179
  64.0 2.3 %step_sizes.7 = (f32[32,2048]{1,0:T(8,128)S(1)}, f32[32,16,128]{2,1,0:T(8,128)S(1)}, f32[32,16,128]{2,1,0:T(8,128)S(1)}) custom-call(f32[32,544]{1,0:T(8,128)S(1)} %copy.107.projected, f32[32,32]{1,0:T(8,128)S(1)} %slice_bitcast_fusion.10.across, f32[1,512]{1,0:T(1,128)S(1)} %bitcast.391, bf16[512,2048]{1,0:T(8,128)(2,1)} %get-tuple-element.379.weight, ...), custom_call_target="tpu_custom_call" | custom-call | flops 1000 | bytes 1000 | tf_op jit(solution)/shard_map/cond/branch_2_fun/step_sizes/pallas_call | solution.py:352
  66.4 27.6 %collective-permute-done.29.xa = bf16[15,16,2048]{2,1,0:T(8,128)(2,1)S(1)} collective-permute-done((bf16[15,16,2048]{2,1,0:T(8,128)(2,1)}, bf16[15,16,2048]{2,1,0:T(8,128)(2,1)S(1)}, u32[]{:S(2)}, u32[]{:S(2)}) %collective-permute-start.29) | collective-permute-done | bytes 983072 | tf_op jit(solution)/shard_map/cond/branch_2_fun/ppermute | solution.py:28
  94.0 8.3 %collective-permute-done.37 = bf16[2,4,4,4096]{3,2,1,0:T(4,128)(2,1)S(1)} collective-permute-done((bf16[2,4,4,4096]{3,2,1,0:T(4,128)(2,1)S(1)}, bf16[2,4,4,4096]{3,2,1,0:T(4,128)(2,1)S(1)}, u32[]{:S(2)}, u32[]{:S(2)}) %collective-permute-start.37) | collective-permute-done | bytes 262176 | tf_op jit(solution)/shard_map/cond/branch_2_fun/ppermute | solution.py:28
  102.8 1.7 %collective-permute-start.36 = (bf16[15,16,2048]{2,1,0:T(8,128)(2,1)S(1)}, bf16[15,16,2048]{2,1,0:T(8,128)(2,1)S(1)}, u32[]{:S(2)}, u32[]{:S(2)}) collective-permute-start(bf16[15,16,2048]{2,1,0:T(8,128)(2,1)S(1)} %collective-permute-done.29.xa), channel_id=1, source_target_pairs={{0,4},{4,0},{8,12},{12,8},{1,5},{5,1},{9,13},{13,9},{2,6},{6,2},{1... | collective-permute-start | bytes 2949128 | tf_op jit(solution)/shard_map/cond/branch_2_fun/ppermute | solution.py:28
  105.3 1.2 collective-permute-start.35
  106.5 7.3 %early.7 = (bf16[32,16,2048]{2,1,0:T(8,128)(2,1)}, f32[32,2048]{1,0:T(8,128)S(1)}, f32[32,2048]{1,0:T(8,128)S(1)}) custom-call(s32[8,128]{1,0:T(8,128)S(1)} %get-tuple-element.841, f32[32,2048]{1,0:T(8,128)S(1)} %get-tuple-element.390.step, f32[32,2048]{1,0:T(8,128)S(1)} %get-tuple-element.391.conv, f32[16,2048]{1,0:T(8,128)S(1)} %copy-done.58, ...), custom_call_target="tpu_custom_call" | custom-call | flops 1000 | bytes 1000 | tf_op jit(solution)/shard_map/cond/branch_2_fun/early/pallas_call | solution.py:451
  114.6 18.4 %collective-permute-done.35.rest_0_ = bf16[5,16,2048]{2,1,0:T(8,128)(2,1)S(1)} collective-permute-done((bf16[5,16,2048]{2,1,0:T(8,128)(2,1)S(1)}, bf16[5,16,2048]{2,1,0:T(8,128)(2,1)S(1)}, u32[]{:S(2)}, u32[]{:S(2)}) %collective-permute-start.35) | collective-permute-done | bytes 327712 | tf_op jit(solution)/shard_map/cond/branch_2_fun/ppermute | solution.py:28
  133.1 2.2 %collective-permute-done.36.rest_1_ = bf16[15,16,2048]{2,1,0:T(8,128)(2,1)S(1)} collective-permute-done((bf16[15,16,2048]{2,1,0:T(8,128)(2,1)S(1)}, bf16[15,16,2048]{2,1,0:T(8,128)(2,1)S(1)}, u32[]{:S(2)}, u32[]{:S(2)}) %collective-permute-start.36) | collective-permute-done | bytes 983072 | tf_op jit(solution)/shard_map/cond/branch_2_fun/ppermute | solution.py:28
  135.3 3.5 %late.7 = (bf16[32,16,2048]{2,1,0:T(8,128)(2,1)}, bf16[32,2048]{1,0:T(8,128)(2,1)}) custom-call(s32[8,128]{1,0:T(8,128)S(1)} %get-tuple-element.841, f32[32,2048]{1,0:T(8,128)S(1)} %get-tuple-element.390.step, f32[32,2048]{1,0:T(8,128)S(1)} %get-tuple-element.391.conv, f32[16,2048]{1,0:T(8,128)S(1)} %copy-done.58, ...), custom_call_target="tpu_custom_call", output_to_operand_aliasing={{0}: (10, {})} | custom-call | flops 1000 | bytes 1000 | tf_op jit(solution)/shard_map/cond/branch_2_fun/late/pallas_call | solution.py:473
  (105 shorter events, 16.5 us)
Async XLA Ops:
  0.6 9.2 %copy-start = (s32[16,8]{0,1:T(8,128)S(1)}, s32[16,8]{0,1:T(8,128)}, u32[]{:S(2)}) copy-start(s32[16,8]{0,1:T(8,128)} %param.42) | copy-start | bytes 1540
  2.1 10.7 %collective-permute-start.66 = (bf16[4,4,1024]{2,0,1:T(4,128)(2,1)S(1)}, bf16[4,4,1024]{2,0,1:T(4,128)(2,1)}, u32[]{:S(2)}, u32[]{:S(2)}) collective-permute-start(bf16[4,4,1024]{2,0,1:T(4,128)(2,1)S(1)} %copy_dynamic-update-slice_fusion), channel_id=1, source_target_pairs={{0,8},{4,12},{8,0},{12,4},{1,9},{5,13},{9,1},{13,5},{2,10},{6,14},... | collective-permute-start | bytes 98312 | tf_op jit(solution)/shard_map/ppermute | solution.py:28
  4.8 8.0 %collective-permute-start.67 = (bf16[4,4,1024]{2,0,1:T(4,128)(2,1)S(1)}, bf16[4,4,1024]{2,0,1:T(4,128)(2,1)}, u32[]{:S(2)}, u32[]{:S(2)}) collective-permute-start(bf16[4,4,1024]{2,0,1:T(4,128)(2,1)S(1)} %copy_dynamic-update-slice_fusion), channel_id=1, source_target_pairs={{0,4},{4,0},{8,12},{12,8},{1,5},{5,1},{9,13},{13,9},{2,6},{6,2},{1... | collective-permute-start | bytes 98312 | tf_op jit(solution)/shard_map/ppermute | solution.py:28
  7.3 8.4 %collective-permute-start.64 = (bf16[4,4,4096]{2,0,1:T(4,128)(2,1)S(1)}, bf16[4,4,4096]{2,0,1:T(4,128)(2,1)}, u32[]{:S(2)}, u32[]{:S(2)}) collective-permute-start(bf16[4,4,4096]{2,0,1:T(4,128)(2,1)S(1)} %copy.120), channel_id=1, source_target_pairs={{0,8},{4,12},{8,0},{12,4},{1,9},{5,13},{9,1},{13,5},{2,10},{6,14},... | collective-permute-start | bytes 393224 | tf_op jit(solution)/shard_map/ppermute | solution.py:28
  7.8 8.0 %collective-permute-start.65 = (bf16[4,4,4096]{2,0,1:T(4,128)(2,1)S(1)}, bf16[4,4,4096]{2,0,1:T(4,128)(2,1)}, u32[]{:S(2)}, u32[]{:S(2)}) collective-permute-start(bf16[4,4,4096]{2,0,1:T(4,128)(2,1)S(1)} %copy.120), channel_id=1, source_target_pairs={{0,4},{4,0},{8,12},{12,8},{1,5},{5,1},{9,13},{13,9},{2,6},{6,2},{1... | collective-permute-start | bytes 393224 | tf_op jit(solution)/shard_map/ppermute | solution.py:28
  16.4 3.7 %copy-start.73 = (s32[4,16,16]{2,1,0:T(8,128)}, s32[4,16,16]{2,1,0:T(8,128)S(1)}, u32[]{:S(2)}) copy-start(s32[4,16,16]{2,1,0:T(8,128)S(1)} %get-tuple-element.874) | copy-start | bytes 12292 | tf_op jit(solution)/shard_map/cond
  19.5 22.3 %collective-permute-start.26 = (bf16[60,2048]{1,0:T(8,128)(2,1)}, bf16[60,2048]{1,0:T(8,128)(2,1)S(1)}, u32[]{:S(2)}, u32[]{:S(2)}) collective-permute-start(bf16[60,2048]{1,0:T(8,128)(2,1)} %get-tuple-element.357), channel_id=1, source_target_pairs={{0,8},{4,12},{8,0},{12,4},{1,9},{5,13},{9,1},{13,5},{2,10},{6,14},... | collective-permute-start | bytes 737288 | tf_op jit(solution)/shard_map/cond/branch_2_fun/ppermute | solution.py:28
  20.1 21.1 %collective-permute-start.27 = (bf16[45,2048]{1,0:T(8,128)(2,1)}, bf16[45,2048]{1,0:T(8,128)(2,1)S(1)}, u32[]{:S(2)}, u32[]{:S(2)}) collective-permute-start(bf16[45,2048]{1,0:T(8,128)(2,1)} %get-tuple-element.358), channel_id=1, source_target_pairs={{0,4},{4,0},{8,12},{12,8},{1,5},{5,1},{9,13},{13,9},{2,6},{6,2},{1... | collective-permute-start | bytes 552968 | tf_op jit(solution)/shard_map/cond/branch_2_fun/ppermute | solution.py:28
  21.2 20.7 %collective-permute-start.28 = (bf16[45,2048]{1,0:T(8,128)(2,1)}, bf16[45,2048]{1,0:T(8,128)(2,1)}, u32[]{:S(2)}, u32[]{:S(2)}) collective-permute-start(bf16[45,2048]{1,0:T(8,128)(2,1)} %get-tuple-element.359), channel_id=1, source_target_pairs={{0,12},{4,8},{8,4},{12,0},{1,13},{5,9},{9,5},{13,1},{2,14},{6,10},... | collective-permute-start | bytes 552968 | tf_op jit(solution)/shard_map/cond/branch_2_fun/ppermute | solution.py:28
  23.9 25.9 %collective-permute-start.31 = (bf16[4,4,4096]{2,0,1:T(4,128)(2,1)}, bf16[4,4,4096]{2,0,1:T(4,128)(2,1)}, u32[]{:S(2)}, u32[]{:S(2)}) collective-permute-start(bf16[4,4,4096]{2,0,1:T(4,128)(2,1)} %get-tuple-element.364), channel_id=1, source_target_pairs={{0,4},{4,0},{8,12},{12,8},{1,5},{5,1},{9,13},{13,9},{2,6},{6,2},{1... | collective-permute-start | bytes 393224 | tf_op jit(solution)/shard_map/cond/branch_2_fun/ppermute | solution.py:28
  23.9 25.9 %collective-permute-start.32 = (bf16[4,4,1024]{2,0,1:T(4,128)(2,1)}, bf16[4,4,1024]{2,0,1:T(4,128)(2,1)}, u32[]{:S(2)}, u32[]{:S(2)}) collective-permute-start(bf16[4,4,1024]{2,0,1:T(4,128)(2,1)} %get-tuple-element.367), channel_id=1, source_target_pairs={{0,4},{4,0},{8,12},{12,8},{1,5},{5,1},{9,13},{13,9},{2,6},{6,2},{1... | collective-permute-start | bytes 98312 | tf_op jit(solution)/shard_map/cond/branch_2_fun/ppermute | solution.py:28
  35.7 6.2 %copy-start.87 = (f32[2048]{0:T(1024)S(1)}, f32[2048]{0:T(1024)}, u32[]{:S(2)}) copy-start(f32[2048]{0:T(1024)} %get-tuple-element.371) | copy-start | bytes 24580 | tf_op jit(solution)/shard_map/cond
  47.0 5.7 %copy-start.103 = (s32[4,16,1]{1,0,2:T(4,128)S(1)}, s32[4,16,1]{1,0,2:T(4,128)}, u32[]{:S(2)}) copy-start(s32[4,16,1]{1,0,2:T(4,128)} %get-tuple-element.802) | copy-start | bytes 772 | tf_op jit(solution)/shard_map/cond
  47.0 5.7 %copy-start.113 = (pred[4,16,1]{1,0,2:T(4,128)(4,1)S(1)}, pred[4,16,1]{1,0,2:T(4,128)(4,1)}, u32[]{:S(2)}) copy-start(pred[4,16,1]{1,0,2:T(4,128)(4,1)} %get-tuple-element.800) | copy-start | bytes 196 | tf_op jit(solution)/shard_map/cond
  47.0 5.7 %copy-start.118 = (s32[4,16]{1,0:T(4,128)S(1)}, s32[4,16]{1,0:T(4,128)}, u32[]{:S(2)}) copy-start(s32[4,16]{1,0:T(4,128)} %select_reduce_fusion.2) | copy-start | bytes 772 | tf_op jit(solution)/shard_map/cond
  48.1 3.3 %collective-permute-start.33 = (f32[32,544]{0,1:T(8,128)S(1)}, f32[32,544]{0,1:T(8,128)S(1)}, u32[]{:S(2)}, u32[]{:S(2)}) collective-permute-start(f32[32,544]{0,1:T(8,128)S(1)} %copy.106), channel_id=1, source_target_pairs={{0,1},{1,0},{2,3},{3,2},{4,5},{5,4},{6,7},{7,6},{8,9},{9,8},{10,11... | collective-permute-start | bytes 208904 | tf_op jit(solution)/shard_map/cond/branch_2_fun/ppermute | solution.py:493
  48.1 45.8 %collective-permute-start.29 = (bf16[15,16,2048]{2,1,0:T(8,128)(2,1)}, bf16[15,16,2048]{2,1,0:T(8,128)(2,1)S(1)}, u32[]{:S(2)}, u32[]{:S(2)}) collective-permute-start(bf16[15,16,2048]{2,1,0:T(8,128)(2,1)} %copy-done.34), channel_id=1, source_target_pairs={{0,8},{4,12},{8,0},{12,4},{1,9},{5,13},{9,1},{13,5},{2,10},{6,14},... | collective-permute-start | bytes 2949128 | tf_op jit(solution)/shard_map/cond/branch_2_fun/ppermute | solution.py:28
  48.2 45.8 %collective-permute-start.30 = (bf16[15,16,2048]{2,1,0:T(8,128)(2,1)}, bf16[15,16,2048]{2,1,0:T(8,128)(2,1)S(1)}, u32[]{:S(2)}, u32[]{:S(2)}) collective-permute-start(bf16[15,16,2048]{2,1,0:T(8,128)(2,1)} %copy-done.33), channel_id=1, source_target_pairs={{0,4},{4,0},{8,12},{12,8},{1,5},{5,1},{9,13},{13,9},{2,6},{6,2},{1... | collective-permute-start | bytes 2949128 | tf_op jit(solution)/shard_map/cond/branch_2_fun/ppermute | solution.py:28
  52.1 10.5 %collective-permute-start.34 = (f32[32,544]{0,1:T(8,128)}, f32[32,544]{0,1:T(8,128)}, u32[]{:S(2)}, u32[]{:S(2)}) collective-permute-start(f32[32,544]{0,1:T(8,128)} %add.178), channel_id=1, source_target_pairs={{0,2},{2,0},{1,3},{3,1},{4,6},{6,4},{5,7},{7,5},{8,10},{10,8},{9,1... | collective-permute-start | bytes 208904 | tf_op jit(solution)/shard_map/cond/branch_2_fun/ppermute | solution.py:493
  52.9 11.1 %copy-start.91 = (f32[2048]{0:T(1024)S(1)}, f32[2048]{0:T(1024)}, u32[]{:S(2)}) copy-start(f32[2048]{0:T(1024)} %get-tuple-element.380) | copy-start | bytes 24580 | tf_op jit(solution)/shard_map/cond
  52.9 11.1 %copy-start.108 = (f32[512]{0:T(512)S(1)}, f32[512]{0:T(512)}, u32[]{:S(2)}) copy-start(f32[512]{0:T(512)} %get-tuple-element.378) | copy-start | bytes 6148 | tf_op jit(solution)/shard_map/cond
  64.0 30.0 %copy-start.50 = (bf16[2,4,4,4096]{3,2,1,0:T(4,128)(2,1)S(1)}, bf16[2,4,4,4096]{3,2,1,0:T(4,128)(2,1)}, u32[]{:S(2)}) copy-start(bf16[2,4,4,4096]{3,2,1,0:T(4,128)(2,1)} %copy-done.49) | copy-start | bytes 786436 | tf_op jit(solution)/shard_map/cond
  64.0 40.6 %copy-start.9 = (bf16[96,2048]{1,0:T(8,128)(2,1)S(1)}, bf16[96,2048]{1,0:T(8,128)(2,1)}, u32[]{:S(2)}) copy-start(bf16[96,2048]{1,0:T(8,128)(2,1)} %copy-done.8) | copy-start | bytes 1179652 | tf_op jit(solution)/shard_map/cond
  64.0 42.5 %copy-start.53 = (bf16[4,8,16,2048]{3,2,1,0:T(8,128)(2,1)S(1)}, bf16[4,8,16,2048]{3,2,1,0:T(8,128)(2,1)}, u32[]{:S(2)}) copy-start(bf16[4,8,16,2048]{3,2,1,0:T(8,128)(2,1)} %get-tuple-element.781) | copy-start | bytes 6291460 | tf_op jit(solution)/shard_map/cond
  66.3 39.0 %copy-start.44 = (bf16[5,16,2048]{2,1,0:T(8,128)(2,1)S(1)}, bf16[5,16,2048]{2,1,0:T(8,128)(2,1)}, u32[]{:S(2)}) copy-start(bf16[5,16,2048]{2,1,0:T(8,128)(2,1)} %copy-done.43) | copy-start | bytes 983044 | tf_op jit(solution)/shard_map/cond
  66.4 40.2 %copy-start.58 = (f32[16,2048]{1,0:T(8,128)S(1)}, f32[16,2048]{1,0:T(8,128)}, u32[]{:S(2)}) copy-start(f32[16,2048]{1,0:T(8,128)} %get-tuple-element.392.decay_log) | copy-start | bytes 393220 | tf_op jit(solution)/shard_map/cond
  66.4 40.2 %copy-start.65 = (bf16[4,8,2048]{2,1,0:T(8,128)(2,1)S(1)}, bf16[4,8,2048]{2,1,0:T(8,128)(2,1)}, u32[]{:S(2)}) copy-start(bf16[4,8,2048]{2,1,0:T(8,128)(2,1)} %get-tuple-element.396) | copy-start | bytes 393220 | tf_op jit(solution)/shard_map/cond
  66.4 40.1 %copy-start.96 = (f32[2048]{0:T(1024)S(1)}, f32[2048]{0:T(1024)}, u32[]{:S(2)}) copy-start(f32[2048]{0:T(1024)} %get-tuple-element.395) | copy-start | bytes 24580 | tf_op jit(solution)/shard_map/cond
  94.0 8.3 %collective-permute-start.37 = (bf16[2,4,4,4096]{3,2,1,0:T(4,128)(2,1)S(1)}, bf16[2,4,4,4096]{3,2,1,0:T(4,128)(2,1)S(1)}, u32[]{:S(2)}, u32[]{:S(2)}) collective-permute-start(bf16[2,4,4,4096]{3,2,1,0:T(4,128)(2,1)S(1)} %copy-done.50), channel_id=1, source_target_pairs={{0,4},{4,0},{8,12},{12,8},{1,5},{5,1},{9,13},{13,9},{2,6},{6,2},{1... | collective-permute-start | bytes 786440 | tf_op jit(solution)/shard_map/cond/branch_2_fun/ppermute | solution.py:28
  102.5 11.3 %collective-permute-start.38 = (bf16[4,4,4096]{2,1,0:T(4,128)(2,1)S(1)}, bf16[4,4,4096]{2,1,0:T(4,128)(2,1)S(1)}, u32[]{:S(2)}, u32[]{:S(2)}) collective-permute-start(bf16[4,4,4096]{2,1,0:T(4,128)(2,1)S(1)} %slice_bitcast_fusion.8), channel_id=1, source_target_pairs={{0,8},{4,12},{8,0},{12,4},{1,9},{5,13},{9,1},{13,5},{2,10},{6,14},... | collective-permute-start | bytes 393224 | tf_op jit(solution)/shard_map/cond/branch_2_fun/ppermute | solution.py:28
  102.8 32.5 %collective-permute-start.36 = (bf16[15,16,2048]{2,1,0:T(8,128)(2,1)S(1)}, bf16[15,16,2048]{2,1,0:T(8,128)(2,1)S(1)}, u32[]{:S(2)}, u32[]{:S(2)}) collective-permute-start(bf16[15,16,2048]{2,1,0:T(8,128)(2,1)S(1)} %collective-permute-done.29.xa), channel_id=1, source_target_pairs={{0,4},{4,0},{8,12},{12,8},{1,5},{5,1},{9,13},{13,9},{2,6},{6,2},{1... | collective-permute-start | bytes 2949128 | tf_op jit(solution)/shard_map/cond/branch_2_fun/ppermute | solution.py:28
  105.3 27.8 %collective-permute-start.35 = (bf16[5,16,2048]{2,1,0:T(8,128)(2,1)S(1)}, bf16[5,16,2048]{2,1,0:T(8,128)(2,1)S(1)}, u32[]{:S(2)}, u32[]{:S(2)}) collective-permute-start(bf16[5,16,2048]{2,1,0:T(8,128)(2,1)S(1)} %copy-done.44), channel_id=1, source_target_pairs={{0,8},{4,12},{8,0},{12,4},{1,9},{5,13},{9,1},{13,5},{2,10},{6,14},... | collective-permute-start | bytes 983048 | tf_op jit(solution)/shard_map/cond/branch_2_fun/ppermute | solution.py:28
  (13 other events, 15.3 us)
